TPU v7x, 32 devices: a whole 2x2x4 slice. The times are simulated.
32 devices in a mesh: particle: 4 (over z), tile: 8 (over y, x, core).
Axes of the slice: x: 2, y: 2, z: 4, core: 2. Of those that a mesh axis runs over, the one named last changes fastest.
Arguments:
- biomass: float32 [16, 32768], P('particle', 'tile'), as said below
- water: float32 [16, 32768], P('particle', 'tile'), may hold values from -5 to 5
- flow_blocks: bfloat16 [256, 3, 128, 128], P('tile'), may hold values from -0.15625 to 0.15625
- neighbours: int32 [256, 3], P('tile'), may hold values from 0 to 255, as said below
- rain: float32 [4, 16, 32768], P(None, 'particle', 'tile'), may hold values from -4 to 4
- growth_rate: float32 [32768], P('tile'), may hold values from 0.05 to 0.5
- observations: float32 [2, 32768], P(None, 'tile'), may hold values from -5 to 5
- obs_precision: float32 [32768], P('tile'), as said below
- ancestors: int32 [2, 16], replicated, may hold values from 0 to 15
Outputs:
- means: float32 [2, 2, 32768], P(None, None, 'tile')
- biomass_out: float32 [16, 32768], P('particle', 'tile')
- water_out: float32 [16, 32768], P('particle', 'tile')
Inputs may be any that keep to these rules, and one draw needn't show every extreme that they name: `neighbours`: row n lists block n first, then one block 1 to 4 blocks below n and one 1 to 4 blocks above n, each clipped to the grid's ends. `biomass`: every entry lies between 0.5 and 2. `obs_precision`: every entry lies between 0.3 / sqrt(32768) and 3 / sqrt(32768).
All inputs are finite; a program needn't handle non-finite values.
Results may differ from a plain program's by a relative error of at most 0.0019.
Values may be sent and summed in bfloat16 or wider, within the bound.
No kernel may reach another device: no remote copies, remote signals or barrier semaphores. Data moves between devices by JAX's collectives and lax.ppermute only.
A program may use at most 64 MiB of HBM per device.

v0:
```python
import jax
import jax.numpy as jnp
from jax import lax
from jax.sharding import PartitionSpec as P

BLK = 128
CYCLES = 2
DAYS = 2
HALO = 4


def padded(cells, sides, width):
    for axis, dim in sides:
        count = lax.axis_size(axis)
        ends = count - 1
        head = lax.slice_in_dim(cells, 0, width, axis=dim)
        tail = lax.slice_in_dim(cells, cells.shape[dim] - width, cells.shape[dim], axis=dim)
        cells = jnp.concatenate(
            [
                lax.ppermute(tail, axis, [(i, (i + 1) % count) for i in range(ends)]),
                cells,
                lax.ppermute(head, axis, [((i + 1) % count, i) for i in range(ends)]),
            ],
            axis=dim,
        )
    return cells


def body(
    biomass,
    water,
    flow_blocks,
    neighbours,
    rain,
    growth_rate,
    observations,
    obs_precision,
    ancestors,
):
    part_dev = biomass.shape[0]
    cells = biomass.shape[1]
    blocks_dev = cells // BLK
    member = lax.axis_index("particle")
    tile_pos = lax.axis_index("tile")
    local_ids = neighbours - tile_pos * blocks_dev + HALO
    bio, wat = (biomass, water)
    collected = []
    for cycle in range(CYCLES):
        misfit_local = -0.5 * jnp.sum(obs_precision * (bio - observations[cycle]) ** 2, axis=1)
        summed = lax.psum(misfit_local, "tile")
        log_weight = lax.all_gather(summed, "particle", axis=0, tiled=True)
        shifted = jnp.exp(log_weight - jnp.max(log_weight))
        weight = shifted / jnp.sum(shifted)
        my_weight = lax.dynamic_slice_in_dim(weight, member * part_dev, part_dev)
        partial_sums = jnp.stack(
            [jnp.sum(my_weight[:, None] * bio, axis=0), jnp.sum(my_weight[:, None] * wat, axis=0)]
        )
        collected.append(lax.psum(partial_sums, "particle"))
        chosen = ancestors[cycle]
        mine = lax.dynamic_slice_in_dim(chosen, member * part_dev, part_dev)
        piece = (
            lax.all_gather(bio, "particle", axis=0, tiled=True),
            lax.all_gather(wat, "particle", axis=0, tiled=True),
        )
        count = piece[0].shape[0]
        hit = jnp.arange(count, dtype=jnp.int32)[None, :] == mine[:, None]
        bio, wat = tuple(
            (jnp.sum(jnp.where(hit[:, :, None], rows[None], 0.0), axis=1) for rows in piece)
        )
        for day in range(DAYS):
            wb = wat.astype(jnp.bfloat16).reshape(part_dev, blocks_dev, BLK)
            extended = padded(wb, (("tile", 1),), HALO)
            nearby = extended[:, local_ids]
            flux = jnp.einsum(
                "pnkc,nkdc->pnd", nearby, flow_blocks, preferred_element_type=jnp.float32
            ).reshape(part_dev, cells)
            wet = wat * wat / (1.0 + wat * wat)
            new_bio = bio + growth_rate * bio * (wet - 0.4 * bio)
            new_wat = wat + flux + rain[cycle * DAYS + day] - 0.2 * bio * wet
            bio = new_bio
            wat = new_wat
    return (jnp.stack(collected), bio, wat)


def solution(mesh):
    placed = (
        P("particle", "tile"),
        P("particle", "tile"),
        P("tile", None, None, None),
        P("tile", None),
        P(None, "particle", "tile"),
        P("tile"),
        P(None, "tile"),
        P("tile"),
        P(),
    )
    return jax.shard_map(
        body,
        mesh=mesh,
        in_specs=placed,
        out_specs=(P(None, None, "tile"), P("particle", "tile"), P("particle", "tile")),
        check_vma=False,
    )
```

profile of v0, /device:TPU:0, one launch (start us, length us, event | category | flops | bytes accessed | tf_op | source)
XLA Modules:
  0.0 191.6 jit_solution(2245552599224987325)
XLA Ops:
  8.2 15.8 %all-gather = f32[4,4,4096]{2,1,0:T(4,128)S(1)} all-gather(f32[1,4,4096]{2,1,0:T(4,128)} %bitcast.146), channel_id=1, replica_groups=mesh['particle'=4,'tile'=8] {'particle'}, dimensions={0}, use_global_device_ids=true | all-gather | bytes 327680 | tf_op jit(solution)/shard_map/all_gather | solution.py:62
  24.8 14.9 %all-gather.1 = f32[4,4,4096]{2,1,0:T(4,128)S(1)} all-gather(f32[1,4,4096]{2,1,0:T(4,128)} %bitcast.152), channel_id=1, replica_groups=mesh['particle'=4,'tile'=8] {'particle'}, dimensions={0}, use_global_device_ids=true | all-gather | bytes 327680 | tf_op jit(solution)/shard_map/all_gather | solution.py:63
  40.5 1.5 select_reduce_fusion.3
  42.0 1.3 collective-permute-start
  43.3 1.3 collective-permute-start.1
  47.1 1.2 dynamic-slice.2
  49.1 1.3 gather_fusion
  50.4 2.9 %multiply_reduce_fusion.5 = (f32[4]{0:T(128)S(1)}, f32[4]{0:T(128)S(1)}, f32[4,4096]{1,0:T(4,128)}, f32[4,4096]{1,0:T(4,128)}, f32[32,4,128,1]{2,1,3,0:T(4,128)S(1)}) fusion(f32[4,4096]{1,0:T(4,128)} %param.9, f32[4096]{0:T(1024)S(1)} %bitcast.156, f32[4096]{0:T(1024)} %param.16, f32[4096]{0:T(1024)S(1)} %bitcast.155, f32[4,4096]{1,0:T(4,128)S(1)} %get-tuple-element.11, ...), kind=kOutput, calls=%fused_computation.50 | convolution fusion | flops 13058040 | bytes 3768352 | tf_op jit(solution)/shard_map/pnkc,nkdc->pnd/dot_general | solution.py:74
  53.4 0.9 fusion.14
  54.9 4.7 %collective-permute-start.2 = (bf16[4,4,128]{2,0,1:T(4,128)(2,1)}, bf16[4,4,128]{2,0,1:T(4,128)(2,1)S(1)}, u32[]{:S(2)}, u32[]{:S(2)}) collective-permute-start(bf16[4,4,128]{2,0,1:T(4,128)(2,1)} %get-tuple-element.27), channel_id=1, source_target_pairs={{0,1},{1,2},{2,3},{3,4},{4,5},{5,6},{6,7},{8,9},{9,10},{10,11},{11... | collective-permute-start | bytes 12296 | tf_op jit(solution)/shard_map/ppermute | solution.py:20
  59.6 1.3 collective-permute-start.3
  61.0 15.7 %all-reduce.2 = (f32[4]{0:T(128)S(1)}, f32[4]{0:T(128)S(1)}) all-reduce(f32[4]{0:T(128)S(1)} %get-tuple-element.38, f32[4]{0:T(128)S(1)} %get-tuple-element.39), channel_id=1, replica_groups=mesh['particle'=4,'tile'=8] {'tile'}, use_global_device_ids=true, to_apply=%region_10.11 | all-reduce | flops 8 | bytes 64 | tf_op jit(solution)/shard_map/psum | solution.py:50
  77.1 11.5 %all-reduce.4 = (f32[16]{0:T(128)S(1)}, f32[16]{0:T(128)S(1)}) all-reduce(f32[16]{0:T(128)S(1)} %dynamic-update-slice.1, f32[16]{0:T(128)S(1)} %dynamic-update-slice), channel_id=1, replica_groups=mesh['particle'=4,'tile'=8] {'particle'}, use_global_device_ids=true, to_apply=%add.1 | all-reduce | flops 32 | bytes 256
  89.3 1.4 fusion.17
  90.7 1.4 broadcast_divide_fusion
  92.7 1.4 fusion.16
  94.1 1.4 broadcast_divide_fusion.1
  96.3 14.1 %all-gather.2 = f32[4,4,4096]{2,1,0:T(4,128)S(1)} all-gather(f32[1,4,4096]{2,1,0:T(4,128)} %bitcast.145), channel_id=1, replica_groups=mesh['particle'=4,'tile'=8] {'particle'}, dimensions={0}, use_global_device_ids=true | all-gather | bytes 327680 | tf_op jit(solution)/shard_map/all_gather | solution.py:62
  113.4 2.1 %multiply_reduce_fusion.1 = (f32[4096]{0:T(1024)S(1)}, f32[4096]{0:T(1024)S(1)}, f32[4,4096]{1,0:T(4,128)S(1)}) fusion(f32[4,4096]{1,0:T(4,128)} %get-tuple-element.21, f32[4]{0:T(128)} %dynamic_slice.14, f32[4,4096]{1,0:T(4,128)} %get-tuple-element.22, f32[4,4096]{1,0:T(4,128)S(1)} %get-tuple-element.11, f32[4,4096]{1,0:T(4,128)S(1)} %get-tuple-element.12, ...), kind=kOutput, calls=%fused_computation.44 | convolution fusion | flops 12902400 | bytes 3686416 | tf_op jit(solution)/shard_map/pnkc,nkdc->pnd/dot_general | solution.py:74
  115.5 13.8 %all-gather.3 = f32[4,4,4096]{2,1,0:T(4,128)S(1)} all-gather(f32[1,4,4096]{2,1,0:T(4,128)S(1)} %bitcast.151), channel_id=1, replica_groups=mesh['particle'=4,'tile'=8] {'particle'}, dimensions={0}, use_global_device_ids=true | all-gather | bytes 327680 | tf_op jit(solution)/shard_map/all_gather | solution.py:63
  130.1 1.5 select_reduce_fusion.1
  131.6 1.3 collective-permute-start.4
  132.9 1.3 collective-permute-start.5
  134.2 1.4 maximum_bitcast_fusion
  137.2 2.7 %multiply_add_fusion = (f32[4,4096]{1,0:T(4,128)}, f32[4,4096]{1,0:T(4,128)S(1)}, f32[32,4,128,1]{2,1,3,0:T(4,128)S(1)}) fusion(f32[4096]{0:T(1024)S(1)} %copy-done.2, f32[4,4096]{1,0:T(4,128)S(1)} %get-tuple-element.5, f32[4,4096]{1,0:T(4,128)S(1)} %get-tuple-element.6, f32[4,4,4096]{2,1,0:T(4,128)} %param.13, bf16[4,32,3,128]{3,0,2,1:T(4,128)(2,1)S(1)} %bitcast.150, ...), kind=kOutput, calls=%fused_computation.41 | convolution fusion | flops 12926976 | bytes 3653632 | tf_op jit(solution)/shard_map/pnkc,nkdc->pnd/dot_general | solution.py:74
  139.9 0.9 fusion.15
  140.8 4.3 %collective-permute-start.6 = (bf16[4,4,128]{2,0,1:T(4,128)(2,1)S(1)}, bf16[4,4,128]{2,0,1:T(4,128)(2,1)S(1)}, u32[]{:S(2)}, u32[]{:S(2)}) collective-permute-start(bf16[4,4,128]{2,0,1:T(4,128)(2,1)S(1)} %get-tuple-element.23), channel_id=1, source_target_pairs={{0,1},{1,2},{2,3},{3,4},{4,5},{5,6},{6,7},{8,9},{9,10},{10,11},{11... | collective-permute-start | bytes 12296 | tf_op jit(solution)/shard_map/ppermute | solution.py:20
  145.1 1.3 collective-permute-start.7
  147.1 1.8 collective-permute-done.7
  149.7 2.7 %fusion.2 = f32[4,4096]{1,0:T(4,128)} fusion(f32[4,4096]{1,0:T(4,128)S(1)} %get-tuple-element.20, bf16[4,32,3,128]{3,0,2,1:T(4,128)(2,1)S(1)} %bitcast.147, bf16[32,3,128,128]{3,2,1,0:T(8,128)(2,1)S(1)} %copy-done, f32[4,4,4096]{2,1,0:T(4,128)} %param.13, f32[4,4096]{1,0:T(4,128)S(1)} %get-tuple-element.5, f32[4,4096]{1,0:T(4,128)S(1)} %get-tuple-element.6, ...), kind=kOutput, calls=%fused_computation.7 | convolution fusion | flops 12845056 | bytes 3588096 | tf_op jit(solution)/shard_map/pnkc,nkdc->pnd/dot_general | solution.py:74
  152.3 31.0 %all-reduce.7.cloned.1.call-done = (f32[1,2,4096]{2,1,0:T(2,128)}, f32[1,2,4096]{2,1,0:T(2,128)}) async-done(((f32[1,2,4096]{2,1,0:T(2,128)}, f32[1,2,4096]{2,1,0:T(2,128)}), (f32[1,2,4096]{2,1,0:T(2,128)}, f32[1,2,4096]{2,1,0:T(2,128)})) %all-reduce.7.cloned.1.call-update) | async-done | bytes 65552 | tf_op jit(solution)/shard_map/psum | solution.py:58
  183.4 1.4 pad_maximum_fusion
  (59 shorter events, 15.2 us)
Async XLA Ops:
  7.2 43.3 %copy-start = (bf16[32,3,128,128]{3,2,1,0:T(8,128)(2,1)S(1)}, bf16[32,3,128,128]{3,2,1,0:T(8,128)(2,1)}, u32[]{:S(2)}) copy-start(bf16[32,3,128,128]{3,2,1,0:T(8,128)(2,1)} %param.11) | copy-start | bytes 9437188
  7.2 176.2 %all-reduce.7.cloned.1.call-start = ((), (), s32[]{:S(2)}) async-start(), calls=%async_computation | async-start | bytes 131072 | tf_op jit(solution)/shard_map/psum | solution.py:58
  24.8 70.7 %copy-start.1 = (f32[4,4096]{1,0:T(4,128)S(1)}, f32[4,4096]{1,0:T(4,128)}, u32[]{:S(2)}) copy-start(f32[4,4096]{1,0:T(4,128)} %param.9) | copy-start | bytes 196612
  24.8 70.7 %copy-start.3 = (f32[4,4096]{1,0:T(4,128)S(1)}, f32[4,4096]{1,0:T(4,128)}, u32[]{:S(2)}) copy-start(f32[4,4096]{1,0:T(4,128)} %param.10) | copy-start | bytes 196612
  42.0 7.0 %collective-permute-start = (bf16[4,4,128]{2,0,1:T(4,128)(2,1)S(1)}, bf16[4,4,128]{2,0,1:T(4,128)(2,1)S(1)}, u32[]{:S(2)}, u32[]{:S(2)}) collective-permute-start(bf16[4,4,128]{2,0,1:T(4,128)(2,1)S(1)} %get-tuple-element.29), channel_id=1, source_target_pairs={{0,1},{1,2},{2,3},{3,4},{4,5},{5,6},{6,7},{8,9},{9,10},{10,11},{11... | collective-permute-start | bytes 12296 | tf_op jit(solution)/shard_map/ppermute | solution.py:20
  43.3 5.7 %collective-permute-start.1 = (bf16[4,4,128]{2,0,1:T(4,128)(2,1)S(1)}, bf16[4,4,128]{2,0,1:T(4,128)(2,1)S(1)}, u32[]{:S(2)}, u32[]{:S(2)}) collective-permute-start(bf16[4,4,128]{2,0,1:T(4,128)(2,1)S(1)} %get-tuple-element.30), channel_id=1, source_target_pairs={{1,0},{2,1},{3,2},{4,3},{5,4},{6,5},{7,6},{9,8},{10,9},{11,10},{12... | collective-permute-start | bytes 12296 | tf_op jit(solution)/shard_map/ppermute | solution.py:22
  54.3 42.0 %copy-start.4 = (bf16[4,32,128]{2,0,1:T(4,128)(2,1)}, bf16[4,32,128]{2,0,1:T(4,128)(2,1)S(1)}, u32[]{:S(2)}) copy-start(bf16[4,32,128]{2,0,1:T(4,128)(2,1)S(1)} %fusion.14) | copy-start | bytes 98308
  54.9 57.0 %collective-permute-start.2 = (bf16[4,4,128]{2,0,1:T(4,128)(2,1)}, bf16[4,4,128]{2,0,1:T(4,128)(2,1)S(1)}, u32[]{:S(2)}, u32[]{:S(2)}) collective-permute-start(bf16[4,4,128]{2,0,1:T(4,128)(2,1)} %get-tuple-element.27), channel_id=1, source_target_pairs={{0,1},{1,2},{2,3},{3,4},{4,5},{5,6},{6,7},{8,9},{9,10},{10,11},{11... | collective-permute-start | bytes 12296 | tf_op jit(solution)/shard_map/ppermute | solution.py:20
  59.6 52.2 %collective-permute-start.3 = (bf16[4,4,128]{2,0,1:T(4,128)(2,1)}, bf16[4,4,128]{2,0,1:T(4,128)(2,1)}, u32[]{:S(2)}, u32[]{:S(2)}) collective-permute-start(bf16[4,4,128]{2,0,1:T(4,128)(2,1)} %get-tuple-element.28), channel_id=1, source_target_pairs={{1,0},{2,1},{3,2},{4,3},{5,4},{6,5},{7,6},{9,8},{10,9},{11,10},{12... | collective-permute-start | bytes 12296 | tf_op jit(solution)/shard_map/ppermute | solution.py:22
  111.8 22.4 %copy-start.5 = (f32[4096]{0:T(1024)S(1)}, f32[4096]{0:T(1024)}, u32[]{:S(2)}) copy-start(f32[4096]{0:T(1024)} %get-tuple-element.7) | copy-start | bytes 49156
  111.8 25.4 %copy-start.2 = (f32[4096]{0:T(1024)S(1)}, f32[4096]{0:T(1024)}, u32[]{:S(2)}) copy-start(f32[4096]{0:T(1024)} %param.14) | copy-start | bytes 49156
  131.6 4.0 %collective-permute-start.4 = (bf16[4,4,128]{2,0,1:T(4,128)(2,1)S(1)}, bf16[4,4,128]{2,0,1:T(4,128)(2,1)S(1)}, u32[]{:S(2)}, u32[]{:S(2)}) collective-permute-start(bf16[4,4,128]{2,0,1:T(4,128)(2,1)S(1)} %get-tuple-element.25), channel_id=1, source_target_pairs={{0,1},{1,2},{2,3},{3,4},{4,5},{5,6},{6,7},{8,9},{9,10},{10,11},{11... | collective-permute-start | bytes 12296 | tf_op jit(solution)/shard_map/ppermute | solution.py:20
  132.9 3.5 %collective-permute-start.5 = (bf16[4,4,128]{2,0,1:T(4,128)(2,1)S(1)}, bf16[4,4,128]{2,0,1:T(4,128)(2,1)S(1)}, u32[]{:S(2)}, u32[]{:S(2)}) collective-permute-start(bf16[4,4,128]{2,0,1:T(4,128)(2,1)S(1)} %get-tuple-element.26), channel_id=1, source_target_pairs={{1,0},{2,1},{3,2},{4,3},{5,4},{6,5},{7,6},{9,8},{10,9},{11,10},{12... | collective-permute-start | bytes 12296 | tf_op jit(solution)/shard_map/ppermute | solution.py:22
  140.8 6.3 %collective-permute-start.6 = (bf16[4,4,128]{2,0,1:T(4,128)(2,1)S(1)}, bf16[4,4,128]{2,0,1:T(4,128)(2,1)S(1)}, u32[]{:S(2)}, u32[]{:S(2)}) collective-permute-start(bf16[4,4,128]{2,0,1:T(4,128)(2,1)S(1)} %get-tuple-element.23), channel_id=1, source_target_pairs={{0,1},{1,2},{2,3},{3,4},{4,5},{5,6},{6,7},{8,9},{9,10},{10,11},{11... | collective-permute-start | bytes 12296 | tf_op jit(solution)/shard_map/ppermute | solution.py:20
  145.1 3.8 %collective-permute-start.7 = (bf16[4,4,128]{2,0,1:T(4,128)(2,1)S(1)}, bf16[4,4,128]{2,0,1:T(4,128)(2,1)S(1)}, u32[]{:S(2)}, u32[]{:S(2)}) collective-permute-start(bf16[4,4,128]{2,0,1:T(4,128)(2,1)S(1)} %get-tuple-element.24), channel_id=1, source_target_pairs={{1,0},{2,1},{3,2},{4,3},{5,4},{6,5},{7,6},{9,8},{10,9},{11,10},{12... | collective-permute-start | bytes 12296 | tf_op jit(solution)/shard_map/ppermute | solution.py:22
Sparse Core Ops, SparseCore 0:
  147.2 36.1 all-reduce.6
where the time goes:
time: 193 us; the launch traced here: 192 us
  blocking collectives  85.8 us (44%)
  waiting for transfers between devices  33.8 us (18%)
  other arithmetic  18.2 us (9%)
  starting transfers between devices  16.8 us (9%)
  between operations  15 us (8%)
  local copies, waits for them, and re-layouts  11.7 us (6%)
  matrix products  10.5 us (5%)
    psum x1, waiting for transfers between devices, body(): collected.append(lax.psum(partial_sums, 'particle'))  31 us
    all_gather x2, blocking collectives, body(): lax.all_gather(bio, 'particle', axis=0, tiled=True)  29.9 us
    all_gather x2, blocking collectives, body(): lax.all_gather(wat, 'particle', axis=0, tiled=True)  28.7 us
    psum x1, blocking collectives, body(): summed = lax.psum(misfit_local, 'tile')  15.7 us
    ppermute x4, starting transfers between devices, padded(): lax.ppermute(tail, axis, [(i, (i + 1) % count) for i in range(ends)])  11.6 us
    unnamed x1, blocking collectives  11.5 us
    dot_general x4, matrix products, body(): jnp.einsum('pnkc,nkdc->pnd', nearby, flow_blocks, preferred_element_type=...  10.5 us
    ppermute x4, starting transfers between devices, padded(): lax.ppermute(head, axis, [((i + 1) % count, i) for i in range(ends)])  5.17 us
  transfers between devices with their start and end apart: 9, of which 3 were waited for; matrix products, arithmetic and copies ran while one was open for 10% of the time, Pallas kernels for 0%

commit v1 on v0

--- a/solution.py
+++ b/solution.py
@@ -7,6 +7,23 @@
 CYCLES = 2
 DAYS = 2
 HALO = 4
+
+
+def joined_along(parts, dim):
+    parts = jnp.moveaxis(parts, 0, dim)
+    shape = parts.shape
+    return parts.reshape(*shape[:dim], shape[dim] * shape[dim + 1], *shape[dim + 2 :])
+
+
+def ring_gather(x, axis, dim):
+    size = lax.axis_size(axis)
+    ahead = [(i, (i + 1) % size) for i in range(size)]
+    blocks = [x]
+    while len(blocks) < size:
+        blocks.append(lax.ppermute(blocks[-1], axis, ahead))
+    index = lax.axis_index(axis)
+    blocks = jnp.stack(blocks)[(index - jnp.arange(size)) % size]
+    return joined_along(blocks, dim)
 
 
 def padded(cells, sides, width):
@@ -60,7 +77,7 @@
         mine = lax.dynamic_slice_in_dim(chosen, member * part_dev, part_dev)
         piece = (
             lax.all_gather(bio, "particle", axis=0, tiled=True),
-            lax.all_gather(wat, "particle", axis=0, tiled=True),
+            ring_gather(wat, "particle", 0),
         )
         count = piece[0].shape[0]
         hit = jnp.arange(count, dtype=jnp.int32)[None, :] == mine[:, None]

time: 193 us -> 216 us (1.12)
  blocking collectives: 85.8 us -> 54 us
  local copies, waits for them, and re-layouts: 11.7 us -> 34.2 us
  other arithmetic: 18.2 us -> 31 us
  waiting for transfers between devices: 33.8 us -> 45.6 us
  starting transfers between devices: 16.8 us -> 22.8 us
    all_gather x2 -> x0, blocking collectives: 28.7 us -> none  [body(): lax.all_gather(wat, 'particle', axis=0, tiled=True)]
    ppermute x0 -> x6, waiting for transfers between devices: none -> 20.1 us  [ring_gather(): blocks.append(lax.ppermute(blocks[-1], axis, ahead))]
    psum x1, waiting for transfers between devices: 31 us -> 23.7 us  [body(): collected.append(lax.psum(partial_sums, 'particle'))]
    ppermute x0 -> x6, starting transfers between devices: none -> 6.55 us  [ring_gather(): blocks.append(lax.ppermute(blocks[-1], axis, ahead))]
    unnamed x21 -> x29, local copies, waits for them, and re-layouts: 4.85 us -> 10.8 us
    gather x4, local copies, waits for them, and re-layouts: 3.43 us -> 8.44 us  [body(): nearby = extended[:, local_ids]]
    concatenate x4, other arithmetic: 0.92 us -> 5.63 us  [padded(): jnp.concatenate([lax.ppermute(tail, axis, [(i, (i + 1) % count) for i in...]
    gather x0 -> x2, local copies, waits for them, and re-layouts: none -> 4.67 us  [ring_gather(): blocks = jnp.stack(blocks)[(index - jnp.arange(size)) % size]]
  transfers between devices with their start and end apart: 9 -> 15, of which waited for: 3 -> 7; matrix products, arithmetic and copies ran while one was open for 10% -> 18% of each run, Pallas kernels for 0% -> 0%
where the time goes in v1:
time: 216 us; the launch traced here: 214 us
  blocking collectives  54 us (25%)
  waiting for transfers between devices  45.6 us (21%)
  local copies, waits for them, and re-layouts  34.2 us (16%)
  other arithmetic  31 us (14%)
  starting transfers between devices  22.8 us (11%)
  between operations  14.8 us (7%)
  matrix products  11.9 us (6%)
    all_gather x2, blocking collectives, body(): lax.all_gather(bio, 'particle', axis=0, tiled=True)  30.2 us
    psum x1, waiting for transfers between devices, body(): collected.append(lax.psum(partial_sums, 'particle'))  23.7 us
    ppermute x6, waiting for transfers between devices, ring_gather(): blocks.append(lax.ppermute(blocks[-1], axis, ahead))  20.1 us
    psum x1, blocking collectives, body(): summed = lax.psum(misfit_local, 'tile')  14.9 us
    dot_general x4, matrix products, body(): jnp.einsum('pnkc,nkdc->pnd', nearby, flow_blocks, preferred_element_type=...  11.9 us
    ppermute x4, starting transfers between devices, padded(): lax.ppermute(tail, axis, [(i, (i + 1) % count) for i in range(ends)])  11.1 us
    unnamed x29, local copies, waits for them, and re-layouts  10.8 us
    unnamed x1, blocking collectives  8.92 us
  transfers between devices with their start and end apart: 15, of which 7 were waited for; matrix products, arithmetic and copies ran while one was open for 18% of the time, Pallas kernels for 0%

profile of v1, /device:TPU:0, one launch (start us, length us, event | category | flops | bytes accessed | tf_op | source)
XLA Modules:
  0.0 214.4 jit_solution(7505295047641305509)
XLA Ops:
  7.2 3.1 %collective-permute-start = (f32[4,4096]{1,0:T(4,128)}, f32[4,4096]{1,0:T(4,128)S(1)}, u32[]{:S(2)}, u32[]{:S(2)}) collective-permute-start(f32[4,4096]{1,0:T(4,128)} %param.10), channel_id=1, source_target_pairs={{0,8},{8,16},{16,24},{24,0},{1,9},{9,17},{17,25},{25,1},{2,10},{10... | collective-permute-start | bytes 196616 | tf_op jit(solution)/shard_map/ppermute | solution.py:23
  14.1 15.0 %all-gather = f32[4,4,4096]{2,1,0:T(4,128)} all-gather(f32[1,4,4096]{2,1,0:T(4,128)} %bitcast.201), channel_id=1, replica_groups=mesh['particle'=4,'tile'=8] {'particle'}, dimensions={0}, use_global_device_ids=true | all-gather | bytes 327680 | tf_op jit(solution)/shard_map/all_gather | solution.py:79
  29.1 1.7 reshape.297
  31.6 6.0 %collective-permute-done.1 = f32[4,4096]{1,0:T(4,128)S(1)} collective-permute-done((f32[4,4096]{1,0:T(4,128)S(1)}, f32[4,4096]{1,0:T(4,128)S(1)}, u32[]{:S(2)}, u32[]{:S(2)}) %collective-permute-start.1) | collective-permute-done | bytes 65568 | tf_op jit(solution)/shard_map/ppermute | solution.py:23
  37.6 6.1 %collective-permute-done.2 = f32[4,4096]{1,0:T(4,128)S(1)} collective-permute-done((f32[4,4096]{1,0:T(4,128)S(1)}, f32[4,4096]{1,0:T(4,128)S(1)}, u32[]{:S(2)}, u32[]{:S(2)}) %collective-permute-start.2) | collective-permute-done | bytes 65568 | tf_op jit(solution)/shard_map/ppermute | solution.py:23
  45.2 2.3 %gather_fusion = f32[4,4,4096]{2,1,0:T(4,128)} fusion(f32[4,4,4096]{2,1,0:T(4,128)} %pad_maximum_fusion, s32[1024]{0:T(1024)S(1)} %pad_clamp_fusion.1), kind=kCustom, calls=%fused_computation | custom fusion | bytes 524304 | tf_op jit(solution)/shard_map/gather | solution.py:25
  47.6 1.7 broadcast_in_dim.84
  59.1 2.1 gather_fusion.1
  61.2 2.9 %multiply_reduce_fusion.5 = (f32[4]{0:T(128)S(1)}, f32[4]{0:T(128)S(1)}, f32[4,4096]{1,0:T(4,128)}, f32[4,4096]{1,0:T(4,128)}, f32[32,4,128,1]{2,1,3,0:T(4,128)S(1)}) fusion(f32[4,4096]{1,0:T(4,128)} %param.9, f32[4096]{0:T(1024)} %bitcast.208, f32[4096]{0:T(1024)} %param.16, f32[4096]{0:T(1024)} %bitcast.207, f32[4,4096]{1,0:T(4,128)S(1)} %get-tuple-element.11, ...), kind=kOutput, calls=%fused_computation.71 | convolution fusion | flops 13058040 | bytes 3768352 | tf_op jit(solution)/shard_map/pnkc,nkdc->pnd/dot_general | solution.py:91
  66.1 4.3 %collective-permute-start.5 = (bf16[4,4,128]{2,0,1:T(4,128)(2,1)}, bf16[4,4,128]{2,0,1:T(4,128)(2,1)S(1)}, u32[]{:S(2)}, u32[]{:S(2)}) collective-permute-start(bf16[4,4,128]{2,0,1:T(4,128)(2,1)} %get-tuple-element.28), channel_id=1, source_target_pairs={{0,1},{1,2},{2,3},{3,4},{4,5},{5,6},{6,7},{8,9},{9,10},{10,11},{11... | collective-permute-start | bytes 12296 | tf_op jit(solution)/shard_map/ppermute | solution.py:37
  72.2 14.9 %all-reduce.2 = (f32[4]{0:T(128)}, f32[4]{0:T(128)}) all-reduce(f32[4]{0:T(128)} %get-tuple-element.39, f32[4]{0:T(128)} %get-tuple-element.40), channel_id=1, replica_groups=mesh['particle'=4,'tile'=8] {'tile'}, use_global_device_ids=true, to_apply=%region_10.11 | all-reduce | flops 8 | bytes 64 | tf_op jit(solution)/shard_map/psum | solution.py:67
  90.8 8.9 %all-reduce.4 = (f32[16]{0:T(128)}, f32[16]{0:T(128)}) all-reduce(f32[16]{0:T(128)} %dynamic-update-slice.1, f32[16]{0:T(128)} %dynamic-update-slice), channel_id=1, replica_groups=mesh['particle'=4,'tile'=8] {'particle'}, use_global_device_ids=true, to_apply=%add.1 | all-reduce | flops 32 | bytes 256
  100.9 1.9 fusion.27
  102.8 2.4 %broadcast_divide_fusion = f32[16]{0:T(128)} fusion(f32[]{:T(128)} %fusion.27, f32[16]{0:T(128)} %get-tuple-element.17, f32[]{:T(128)} %reduce_max.19), kind=kLoop, calls=%fused_computation.95 | loop fusion | flops 32 | bytes 136 | tf_op jit(solution)/shard_map/div | solution.py:70
  106.5 1.8 fusion.26
  108.3 1.9 broadcast_divide_fusion.1
  114.6 2.1 gather_fusion.2
  116.7 3.4 %multiply_reduce_fusion.1 = (f32[4096]{0:T(1024)}, f32[4096]{0:T(1024)}, f32[4,4096]{1,0:T(4,128)S(1)}, f32[32,4,128,1]{2,1,3,0:T(4,128)}) fusion(f32[4,4096]{1,0:T(4,128)} %get-tuple-element.22, f32[4]{0:T(128)} %dynamic_slice.14, f32[4,4096]{1,0:T(4,128)} %get-tuple-element.23, f32[4,4096]{1,0:T(4,128)S(1)} %get-tuple-element.11, ...), kind=kOutput, calls=%fused_computation.65 | convolution fusion | flops 12902400 | bytes 3751952 | tf_op jit(solution)/shard_map/pnkc,nkdc->pnd/dot_general | solution.py:91
  120.2 2.0 collective-permute-start.7
  122.8 3.6 %collective-permute-done.7 = f32[4,4096]{1,0:T(4,128)} collective-permute-done((f32[4,4096]{1,0:T(4,128)S(1)}, f32[4,4096]{1,0:T(4,128)}, u32[]{:S(2)}, u32[]{:S(2)}) %collective-permute-start.7) | collective-permute-done | bytes 65568 | tf_op jit(solution)/shard_map/ppermute | solution.py:23
  127.0 15.1 %all-gather.1 = f32[4,4,4096]{2,1,0:T(4,128)} all-gather(f32[1,4,4096]{2,1,0:T(4,128)S(1)} %bitcast.200), channel_id=1, replica_groups=mesh['particle'=4,'tile'=8] {'particle'}, dimensions={0}, use_global_device_ids=true | all-gather | bytes 327680 | tf_op jit(solution)/shard_map/all_gather | solution.py:79
  142.2 1.7 reshape.299
  145.7 4.5 %collective-permute-done.9 = f32[4,4096]{1,0:T(4,128)S(1)} collective-permute-done((f32[4,4096]{1,0:T(4,128)}, f32[4,4096]{1,0:T(4,128)S(1)}, u32[]{:S(2)}, u32[]{:S(2)}) %collective-permute-start.9) | collective-permute-done | bytes 65568 | tf_op jit(solution)/shard_map/ppermute | solution.py:23
  150.2 1.6 pad_maximum_fusion.1
  151.8 2.3 %gather_fusion.3 = f32[4,4,4096]{2,1,0:T(4,128)} fusion(f32[4,4,4096]{2,1,0:T(4,128)} %pad_maximum_fusion.1, s32[1024]{0:T(1024)S(1)} %pad_clamp_fusion.1), kind=kCustom, calls=%fused_computation.3 | custom fusion | bytes 524304 | tf_op jit(solution)/shard_map/gather | solution.py:25
  154.2 1.7 broadcast_in_dim.89
  164.4 2.1 gather_fusion.4
  166.5 2.8 %multiply_add_fusion = (f32[4,4096]{1,0:T(4,128)}, f32[4,4096]{1,0:T(4,128)}, f32[32,4,128,1]{2,1,3,0:T(4,128)S(1)}) fusion(f32[4096]{0:T(1024)} %param.14, f32[4,4096]{1,0:T(4,128)S(1)} %get-tuple-element.5, f32[4,4096]{1,0:T(4,128)S(1)} %get-tuple-element.6, f32[4,4,4096]{2,1,0:T(4,128)S(1)} %copy-done.1, bf16[4,32,3,128]{3,0,2,1:T(4,128)(2,1)} %bitcast.205, ...), kind=kOutput, calls=%fused_computation.62 | convolution fusion | flops 12926976 | bytes 3653632 | tf_op jit(solution)/shard_map/pnkc,nkdc->pnd/dot_general | solution.py:91
  170.5 4.3 %collective-permute-start.12 = (bf16[4,4,128]{2,0,1:T(4,128)(2,1)}, bf16[4,4,128]{2,0,1:T(4,128)(2,1)S(1)}, u32[]{:S(2)}, u32[]{:S(2)}) collective-permute-start(bf16[4,4,128]{2,0,1:T(4,128)(2,1)} %get-tuple-element.24), channel_id=1, source_target_pairs={{0,1},{1,2},{2,3},{3,4},{4,5},{5,6},{6,7},{8,9},{9,10},{10,11},{11... | collective-permute-start | bytes 12296 | tf_op jit(solution)/shard_map/ppermute | solution.py:37
  176.1 23.7 %all-reduce.7.cloned.1.call-done = (f32[1,2,4096]{2,1,0:T(2,128)}, f32[1,2,4096]{2,1,0:T(2,128)}) async-done(((f32[1,2,4096]{2,1,0:T(2,128)}, f32[1,2,4096]{2,1,0:T(2,128)}), (f32[1,2,4096]{2,1,0:T(2,128)}, f32[1,2,4096]{2,1,0:T(2,128)})) %all-reduce.7.cloned.1.call-update) | async-done | bytes 65552 | tf_op jit(solution)/shard_map/psum | solution.py:75
  202.7 2.1 gather_fusion.5
  204.8 2.8 %fusion.2 = f32[4,4096]{1,0:T(4,128)} fusion(f32[4,4096]{1,0:T(4,128)} %get-tuple-element.20, bf16[4,32,3,128]{3,0,2,1:T(4,128)(2,1)} %bitcast.202, bf16[32,3,128,128]{3,2,1,0:T(8,128)(2,1)S(1)} %copy-done, f32[4,4,4096]{2,1,0:T(4,128)S(1)} %copy-done.1, f32[4,4096]{1,0:T(4,128)S(1)} %get-tuple-element.5, f32[4,4096]{1,0:T(4,128)S(1)} %get-tuple-element.6, ...), kind=kOutput, calls=%fused_computation.9 | convolution fusion | flops 12845056 | bytes 3588096 | tf_op jit(solution)/shard_map/pnkc,nkdc->pnd/dot_general | solution.py:91
  (86 shorter events, 46.5 us)
Async XLA Ops:
  7.2 54.1 %copy-start = (bf16[32,3,128,128]{3,2,1,0:T(8,128)(2,1)S(1)}, bf16[32,3,128,128]{3,2,1,0:T(8,128)(2,1)}, u32[]{:S(2)}) copy-start(bf16[32,3,128,128]{3,2,1,0:T(8,128)(2,1)} %param.11) | copy-start | bytes 9437188
  7.2 54.1 %copy-start.1 = (f32[4,4,4096]{2,1,0:T(4,128)S(1)}, f32[4,4,4096]{2,1,0:T(4,128)}, u32[]{:S(2)}) copy-start(f32[4,4,4096]{2,1,0:T(4,128)} %param.13) | copy-start | bytes 786436
  7.2 192.6 %all-reduce.7.cloned.1.call-start = ((), (), s32[]{:S(2)}) async-start(), calls=%async_computation | async-start | bytes 131072 | tf_op jit(solution)/shard_map/psum | solution.py:75
  7.2 24.3 %collective-permute-start = (f32[4,4096]{1,0:T(4,128)}, f32[4,4096]{1,0:T(4,128)S(1)}, u32[]{:S(2)}, u32[]{:S(2)}) collective-permute-start(f32[4,4096]{1,0:T(4,128)} %param.10), channel_id=1, source_target_pairs={{0,8},{8,16},{16,24},{24,0},{1,9},{9,17},{17,25},{25,1},{2,10},{10... | collective-permute-start | bytes 196616 | tf_op jit(solution)/shard_map/ppermute | solution.py:23
  31.5 6.1 %collective-permute-start.1 = (f32[4,4096]{1,0:T(4,128)S(1)}, f32[4,4096]{1,0:T(4,128)S(1)}, u32[]{:S(2)}, u32[]{:S(2)}) collective-permute-start(f32[4,4096]{1,0:T(4,128)S(1)} %collective-permute-done), channel_id=1, source_target_pairs={{0,8},{8,16},{16,24},{24,0},{1,9},{9,17},{17,25},{25,1},{2,10},{10... | collective-permute-start | bytes 196616 | tf_op jit(solution)/shard_map/ppermute | solution.py:23
  37.6 6.1 %collective-permute-start.2 = (f32[4,4096]{1,0:T(4,128)S(1)}, f32[4,4096]{1,0:T(4,128)S(1)}, u32[]{:S(2)}, u32[]{:S(2)}) collective-permute-start(f32[4,4096]{1,0:T(4,128)S(1)} %collective-permute-done.1), channel_id=1, source_target_pairs={{0,8},{8,16},{16,24},{24,0},{1,9},{9,17},{17,25},{25,1},{2,10},{10... | collective-permute-start | bytes 196616 | tf_op jit(solution)/shard_map/ppermute | solution.py:23
  50.8 1.9 copy-start.5
  51.4 4.9 %collective-permute-start.3 = (bf16[4,4,128]{2,0,1:T(4,128)(2,1)}, bf16[4,4,128]{2,0,1:T(4,128)(2,1)S(1)}, u32[]{:S(2)}, u32[]{:S(2)}) collective-permute-start(bf16[4,4,128]{2,0,1:T(4,128)(2,1)} %get-tuple-element.30), channel_id=1, source_target_pairs={{0,1},{1,2},{2,3},{3,4},{4,5},{5,6},{6,7},{8,9},{9,10},{10,11},{11... | collective-permute-start | bytes 12296 | tf_op jit(solution)/shard_map/ppermute | solution.py:37
  52.7 5.0 %collective-permute-start.4 = (bf16[4,4,128]{2,0,1:T(4,128)(2,1)}, bf16[4,4,128]{2,0,1:T(4,128)(2,1)S(1)}, u32[]{:S(2)}, u32[]{:S(2)}) collective-permute-start(bf16[4,4,128]{2,0,1:T(4,128)(2,1)} %get-tuple-element.31), channel_id=1, source_target_pairs={{1,0},{2,1},{3,2},{4,3},{5,4},{6,5},{7,6},{9,8},{10,9},{11,10},{12... | collective-permute-start | bytes 12296 | tf_op jit(solution)/shard_map/ppermute | solution.py:39
  64.2 0.6 copy-start.3
  64.9 0.6 copy-start.4
  66.1 47.1 %collective-permute-start.5 = (bf16[4,4,128]{2,0,1:T(4,128)(2,1)}, bf16[4,4,128]{2,0,1:T(4,128)(2,1)S(1)}, u32[]{:S(2)}, u32[]{:S(2)}) collective-permute-start(bf16[4,4,128]{2,0,1:T(4,128)(2,1)} %get-tuple-element.28), channel_id=1, source_target_pairs={{0,1},{1,2},{2,3},{3,4},{4,5},{5,6},{6,7},{8,9},{9,10},{10,11},{11... | collective-permute-start | bytes 12296 | tf_op jit(solution)/shard_map/ppermute | solution.py:37
  70.3 42.9 %collective-permute-start.6 = (bf16[4,4,128]{2,0,1:T(4,128)(2,1)}, bf16[4,4,128]{2,0,1:T(4,128)(2,1)S(1)}, u32[]{:S(2)}, u32[]{:S(2)}) collective-permute-start(bf16[4,4,128]{2,0,1:T(4,128)(2,1)} %get-tuple-element.29), channel_id=1, source_target_pairs={{1,0},{2,1},{3,2},{4,3},{5,4},{6,5},{7,6},{9,8},{10,9},{11,10},{12... | collective-permute-start | bytes 12296 | tf_op jit(solution)/shard_map/ppermute | solution.py:39
  116.7 5.4 %copy-start.8 = (f32[4096]{0:T(1024)S(1)}, f32[4096]{0:T(1024)}, u32[]{:S(2)}) copy-start(f32[4096]{0:T(1024)} %get-tuple-element.7) | copy-start | bytes 49156
  116.7 5.4 %copy-start.9 = (f32[4096]{0:T(1024)S(1)}, f32[4096]{0:T(1024)}, u32[]{:S(2)}) copy-start(f32[4096]{0:T(1024)} %get-tuple-element.8) | copy-start | bytes 49156
  116.7 10.3 %copy-start.2 = (f32[4,4096]{1,0:T(4,128)S(1)}, f32[4,4096]{1,0:T(4,128)}, u32[]{:S(2)}) copy-start(f32[4,4096]{1,0:T(4,128)} %get-tuple-element.22) | copy-start | bytes 196612
  116.7 39.1 %copy-start.10 = (pred[4,16]{1,0:T(4,128)(4,1)S(1)}, pred[4,16]{1,0:T(4,128)(4,1)}, u32[]{:S(2)}) copy-start(pred[4,16]{1,0:T(4,128)(4,1)} %iota_compare_fusion) | copy-start | bytes 196
  120.2 6.2 %collective-permute-start.7 = (f32[4,4096]{1,0:T(4,128)S(1)}, f32[4,4096]{1,0:T(4,128)}, u32[]{:S(2)}, u32[]{:S(2)}) collective-permute-start(f32[4,4096]{1,0:T(4,128)S(1)} %get-tuple-element.21), channel_id=1, source_target_pairs={{0,8},{8,16},{16,24},{24,0},{1,9},{9,17},{17,25},{25,1},{2,10},{10... | collective-permute-start | bytes 196616 | tf_op jit(solution)/shard_map/ppermute | solution.py:23
  126.4 17.5 %collective-permute-start.8 = (f32[4,4096]{1,0:T(4,128)}, f32[4,4096]{1,0:T(4,128)}, u32[]{:S(2)}, u32[]{:S(2)}) collective-permute-start(f32[4,4096]{1,0:T(4,128)} %collective-permute-done.7), channel_id=1, source_target_pairs={{0,8},{8,16},{16,24},{24,0},{1,9},{9,17},{17,25},{25,1},{2,10},{10... | collective-permute-start | bytes 196616 | tf_op jit(solution)/shard_map/ppermute | solution.py:23
  143.9 6.3 %collective-permute-start.9 = (f32[4,4096]{1,0:T(4,128)}, f32[4,4096]{1,0:T(4,128)S(1)}, u32[]{:S(2)}, u32[]{:S(2)}) collective-permute-start(f32[4,4096]{1,0:T(4,128)} %collective-permute-done.8), channel_id=1, source_target_pairs={{0,8},{8,16},{16,24},{24,0},{1,9},{9,17},{17,25},{25,1},{2,10},{10... | collective-permute-start | bytes 196616 | tf_op jit(solution)/shard_map/ppermute | solution.py:23
  157.4 0.6 copy-start.6
  158.6 4.0 %collective-permute-start.10 = (bf16[4,4,128]{2,0,1:T(4,128)(2,1)}, bf16[4,4,128]{2,0,1:T(4,128)(2,1)S(1)}, u32[]{:S(2)}, u32[]{:S(2)}) collective-permute-start(bf16[4,4,128]{2,0,1:T(4,128)(2,1)} %get-tuple-element.26), channel_id=1, source_target_pairs={{0,1},{1,2},{2,3},{3,4},{4,5},{5,6},{6,7},{8,9},{9,10},{10,11},{11... | collective-permute-start | bytes 12296 | tf_op jit(solution)/shard_map/ppermute | solution.py:37
  159.9 3.1 %collective-permute-start.11 = (bf16[4,4,128]{2,0,1:T(4,128)(2,1)S(1)}, bf16[4,4,128]{2,0,1:T(4,128)(2,1)S(1)}, u32[]{:S(2)}, u32[]{:S(2)}) collective-permute-start(bf16[4,4,128]{2,0,1:T(4,128)(2,1)S(1)} %get-tuple-element.27), channel_id=1, source_target_pairs={{1,0},{2,1},{3,2},{4,3},{5,4},{6,5},{7,6},{9,8},{10,9},{11,10},{12... | collective-permute-start | bytes 12296 | tf_op jit(solution)/shard_map/ppermute | solution.py:39
  169.3 0.6 copy-start.7
  170.5 30.7 %collective-permute-start.12 = (bf16[4,4,128]{2,0,1:T(4,128)(2,1)}, bf16[4,4,128]{2,0,1:T(4,128)(2,1)S(1)}, u32[]{:S(2)}, u32[]{:S(2)}) collective-permute-start(bf16[4,4,128]{2,0,1:T(4,128)(2,1)} %get-tuple-element.24), channel_id=1, source_target_pairs={{0,1},{1,2},{2,3},{3,4},{4,5},{5,6},{6,7},{8,9},{9,10},{10,11},{11... | collective-permute-start | bytes 12296 | tf_op jit(solution)/shard_map/ppermute | solution.py:37
  174.8 26.5 %collective-permute-start.13 = (bf16[4,4,128]{2,0,1:T(4,128)(2,1)S(1)}, bf16[4,4,128]{2,0,1:T(4,128)(2,1)S(1)}, u32[]{:S(2)}, u32[]{:S(2)}) collective-permute-start(bf16[4,4,128]{2,0,1:T(4,128)(2,1)S(1)} %get-tuple-element.25), channel_id=1, source_target_pairs={{1,0},{2,1},{3,2},{4,3},{5,4},{6,5},{7,6},{9,8},{10,9},{11,10},{12... | collective-permute-start | bytes 12296 | tf_op jit(solution)/shard_map/ppermute | solution.py:39
Sparse Core Ops, SparseCore 0:
  162.7 37.0 all-reduce.6
